TPU v7x, 256 devices: a whole 4x4x8 slice. The times are simulated.
256 devices in a mesh: expert: 64 (over z, x_lo, y), dp: 4 (over x_hi, core).
Axes of the slice: x: 4 (x_hi: 2, x_lo: 2; x = x_hi * 2 + x_lo), y: 4, z: 8, core: 2. Of those that a mesh axis runs over, the one named last changes fastest.
Arguments:
- tokens: bfloat16 [32768, 2048], P(('expert', 'dp')), may hold values from -6 to 6
- cotangent: bfloat16 [32768, 2048], P(('expert', 'dp')), may hold values from -0.59765625 to 0.59765625
- routes: int32 [32768, 2], P(('expert', 'dp')), may hold values from 0 to 63, as said below
- combine: float32 [32768, 2], P(('expert', 'dp')), may hold values from 0.2 to 1
- counts: int32 [64], replicated, may hold values from 0 to 2999, as said below
- gate_weight: bfloat16 [64, 2048, 512], P('expert'), may hold values from -0.125 to 0.125
- up_weight: bfloat16 [64, 2048, 512], P('expert'), may hold values from -0.125 to 0.125
- down_weight: bfloat16 [64, 2048, 512], P('expert'), may hold values from -0.25 to 0.25
Outputs:
- mixed: bfloat16 [32768, 2048], P(('expert', 'dp'))
- input_grad: bfloat16 [32768, 2048], P(('expert', 'dp'))
- combine_grad: float32 [32768, 2], P(('expert', 'dp'))
- gate_grad: float32 [64, 2048, 512], P('expert', None, 'dp')
- up_grad: float32 [64, 2048, 512], P('expert', None, 'dp')
- down_grad: float32 [64, 2048, 512], P('expert', None, 'dp')
Inputs may be any that keep to these rules, and one draw needn't show every extreme that they name: `counts`: the two largest entries are unique: no other expert has a count equal to either. `routes`: rows come in aligned blocks of 128, one block to a device. In a block the two experts of a row differ. One and the same expert other than the two with the largest counts is named exactly 4 + 4 // 2 times in every block; every other such expert at most 4 times. Each of the two with the largest counts is named at least 8 and at most 12 + 4 // 2 times in a block, and that most in some block.
All inputs are finite; a program needn't handle non-finite values.
Results may differ from a plain program's by a relative error of at most 0.0065.
Values may be sent and summed in bfloat16 or wider, within the bound.
No kernel may reach another device: no remote copies, remote signals or barrier semaphores. Data moves between devices by JAX's collectives and lax.ppermute only.
A program may use at most 128 MiB of HBM per device.

v0:
```python
import jax
import jax.numpy as jnp
from jax import lax
from jax.sharding import PartitionSpec as P


def spread(array, axis, root):
    mine = lax.axis_index(axis) == root
    return lax.psum(jnp.where(mine, array, jnp.zeros_like(array)), axis)


def slot_owners(slot_index, slot_total, positions):
    matches = slot_index[None, :] == jnp.arange(slot_total, dtype=jnp.int32)[:, None]
    occupied = jnp.any(matches, axis=1)
    filler = jnp.sum(jnp.where(matches, positions[None, :], 0), axis=1)
    return (filler, occupied)


def route_plan(routes, hot_ids, experts, capacity, hot_cap):
    flat_routes = routes.reshape(-1)
    pair_count = flat_routes.shape[0]
    expert_ids = jnp.arange(experts, dtype=jnp.int32)
    onehot = (flat_routes[:, None] == expert_ids[None, :]).astype(jnp.int32)
    running = jnp.cumsum(onehot, axis=0)
    slot_rank = jnp.sum((running - onehot) * onehot, axis=1)
    leading = flat_routes == hot_ids[0]
    trailing = flat_routes == hot_ids[1]
    is_hot = leading | trailing
    keep_mask = slot_rank < jnp.where(is_hot, hot_cap, capacity)
    main_total = experts * capacity
    hot_total = 2 * hot_cap
    main_index = jnp.where(keep_mask & ~is_hot, flat_routes * capacity + slot_rank, main_total)
    hot_index = jnp.where(keep_mask & is_hot, jnp.where(leading, 0, hot_cap) + slot_rank, hot_total)
    assign = jnp.where(
        keep_mask, jnp.where(is_hot, main_total + hot_index, main_index), main_total + hot_total
    )
    positions = jnp.arange(pair_count, dtype=jnp.int32)
    main_fill, main_used = slot_owners(main_index, main_total, positions)
    hot_fill, hot_used = slot_owners(hot_index, hot_total, positions)
    return (main_fill, main_used, hot_fill, hot_used, assign)


def expert_forward(row_data, gate_weight, up_weight, down_weight):
    gate_value = jnp.dot(row_data, gate_weight, preferred_element_type=jnp.float32)
    up_value = jnp.dot(row_data, up_weight, preferred_element_type=jnp.float32)
    sigmoid_gate = jax.nn.sigmoid(gate_value)
    activation = (gate_value * sigmoid_gate * up_value).astype(jnp.bfloat16)
    output = lax.dot_general(
        activation, down_weight, (((1,), (1,)), ((), ())), preferred_element_type=jnp.float32
    )
    return ((gate_value, up_value, sigmoid_gate, activation), output)


def expert_backward(cot_rows, stored, gate_weight, up_weight, down_weight):
    gate_value, up_value, sigmoid_gate, activation = stored
    back_hidden = jnp.dot(cot_rows, down_weight, preferred_element_type=jnp.float32)
    gate_part = (
        back_hidden * up_value * sigmoid_gate * (1.0 + gate_value * (1.0 - sigmoid_gate))
    ).astype(jnp.bfloat16)
    up_part = (back_hidden * gate_value * sigmoid_gate).astype(jnp.bfloat16)
    contract_last = (((1,), (1,)), ((), ()))
    input_part = lax.dot_general(
        gate_part, gate_weight, contract_last, preferred_element_type=jnp.float32
    ) + lax.dot_general(up_part, up_weight, contract_last, preferred_element_type=jnp.float32)
    return (gate_part, up_part, input_part)


def weight_grads(row_data, cot_rows, activation, gate_part, up_part):
    contract_rows = (((0,), (0,)), ((), ()))
    return jnp.stack(
        [
            lax.dot_general(row_data, gate_part, contract_rows, preferred_element_type=jnp.float32),
            lax.dot_general(row_data, up_part, contract_rows, preferred_element_type=jnp.float32),
            lax.dot_general(
                cot_rows, activation, contract_rows, preferred_element_type=jnp.float32
            ),
        ]
    )


def per_device(tokens, cotangent, routes, combine, counts, gate_weight, up_weight, down_weight):
    experts = lax.axis_size("expert")
    groups = lax.axis_size("dp")
    tok_count = tokens.shape[0]
    model_width = tokens.shape[1]
    hidden = gate_weight.shape[2]
    hidden_share = hidden // groups
    capacity = 2 * tok_count // experts
    hot_cap = 3 * capacity
    hot_ids = lax.top_k(counts, 2)[1]
    main_fill, main_used, hot_fill, hot_used, assign = route_plan(
        routes, hot_ids, experts, capacity, hot_cap
    )
    flat_combine = combine.reshape(-1)
    zero_value = jnp.zeros((), jnp.bfloat16)

    def pack_rows(filler, occupied):
        token_index = filler // 2
        row_mask = occupied[:, None]
        row_data = jnp.where(row_mask, tokens[token_index], zero_value)
        scaled = (
            flat_combine[filler][:, None] * cotangent[token_index].astype(jnp.float32)
        ).astype(jnp.bfloat16)
        return (row_data, jnp.where(row_mask, scaled, zero_value))

    send_data, send_cot = pack_rows(main_fill, main_used)
    send_data = send_data.reshape(experts, capacity, model_width)
    send_cot = send_cot.reshape(experts, capacity, model_width)
    weights = (gate_weight[0], up_weight[0], down_weight[0])
    got_data = lax.all_to_all(send_data, "expert", split_axis=0, concat_axis=0, tiled=True).reshape(
        -1, model_width
    )
    stored, output = expert_forward(got_data, *weights)
    back_out = lax.all_to_all(
        output.astype(jnp.bfloat16).reshape(experts, capacity, model_width),
        "expert",
        split_axis=0,
        concat_axis=0,
        tiled=True,
    )
    got_cot = lax.all_to_all(send_cot, "expert", split_axis=0, concat_axis=0, tiled=True).reshape(
        -1, model_width
    )
    gate_part, up_part, input_part = expert_backward(got_cot, stored, *weights)
    back_input = lax.all_to_all(
        input_part.astype(jnp.bfloat16).reshape(experts, capacity, model_width),
        "expert",
        split_axis=0,
        concat_axis=0,
        tiled=True,
    )
    group_index = lax.axis_index("dp")
    own_slices = jnp.stack(
        [
            lax.dynamic_slice_in_dim(matrix[0], group_index * hidden_share, hidden_share, 1)
            for matrix in (gate_weight, up_weight, down_weight)
        ]
    )
    hot_weights = [spread(own_slices, "expert", hot_ids[member]) for member in range(2)]
    hot_data, hot_cot = pack_rows(hot_fill, hot_used)
    hot_data = hot_data.reshape(2, hot_cap, model_width)
    hot_cot = hot_cot.reshape(2, hot_cap, model_width)

    def hot_forward(all_data):
        results = [
            expert_forward(
                all_data[member],
                hot_weights[member][0],
                hot_weights[member][1],
                hot_weights[member][2],
            )
            for member in range(2)
        ]
        return ([entry[0] for entry in results], jnp.stack([entry[1] for entry in results]))

    def hot_backward(all_cot, hot_stored):
        results = [
            expert_backward(
                all_cot[member],
                hot_stored[member],
                hot_weights[member][0],
                hot_weights[member][1],
                hot_weights[member][2],
            )
            for member in range(2)
        ]
        return (results, jnp.stack([entry[2] for entry in results]))

    all_data = lax.all_gather(hot_data, "dp", axis=1, tiled=True)
    hot_stored, hot_partial = hot_forward(all_data)
    hot_out = lax.psum_scatter(hot_partial, "dp", scatter_dimension=1, tiled=True)
    all_cot = lax.all_gather(hot_cot, "dp", axis=1, tiled=True)
    hot_parts, hot_input_partial = hot_backward(all_cot, hot_stored)
    hot_input = lax.psum_scatter(hot_input_partial, "dp", scatter_dimension=1, tiled=True)
    shadow = jnp.stack(
        [
            weight_grads(
                all_data[member],
                all_cot[member],
                hot_stored[member][3],
                hot_parts[member][0],
                hot_parts[member][1],
            )
            for member in range(2)
        ]
    )
    summed = lax.psum(shadow, "expert")
    owner_mask = (hot_ids == lax.axis_index("expert")).astype(jnp.float32)
    shadow_part = owner_mask[0] * summed[0] + owner_mask[1] * summed[1]
    own_grads = lax.psum_scatter(
        weight_grads(got_data, got_cot, stored[3], gate_part, up_part),
        "dp",
        scatter_dimension=2,
        tiled=True,
    )
    grad_total = own_grads + shadow_part
    zero_row = jnp.zeros((1, model_width), jnp.bfloat16)
    out_table = jnp.concatenate(
        [
            back_out.reshape(-1, model_width),
            hot_out.astype(jnp.bfloat16).reshape(-1, model_width),
            zero_row,
        ],
        axis=0,
    )
    input_table = jnp.concatenate(
        [
            back_input.reshape(-1, model_width),
            hot_input.astype(jnp.bfloat16).reshape(-1, model_width),
            zero_row,
        ],
        axis=0,
    )
    out_each = out_table[assign].reshape(tok_count, 2, model_width).astype(jnp.float32)
    mixed = jnp.sum(combine[:, :, None] * out_each, axis=1).astype(jnp.bfloat16)
    combine_grad = jnp.sum(out_each * cotangent.astype(jnp.float32)[:, None, :], axis=2)
    input_each = input_table[assign].reshape(tok_count, 2, model_width).astype(jnp.float32)
    input_grad = jnp.sum(input_each, axis=1).astype(jnp.bfloat16)
    return (
        mixed,
        input_grad,
        combine_grad,
        grad_total[0][None],
        grad_total[1][None],
        grad_total[2][None],
    )


def solution(mesh):
    placed = (
        P(("expert", "dp"), None),
        P(("expert", "dp"), None),
        P(("expert", "dp"), None),
        P(("expert", "dp"), None),
        P(),
        P("expert", None, None),
        P("expert", None, None),
        P("expert", None, None),
    )
    return jax.shard_map(
        per_device,
        mesh=mesh,
        in_specs=placed,
        out_specs=(
            P(("expert", "dp"), None),
            P(("expert", "dp"), None),
            P(("expert", "dp"), None),
            P("expert", None, "dp"),
            P("expert", None, "dp"),
            P("expert", None, "dp"),
        ),
        check_vma=False,
    )
```

profile of v0, /device:TPU:4, one launch (start us, length us, event | category | flops | bytes accessed | tf_op | source)
XLA Modules:
  0.0 1377.4 jit_solution(5303750272594557895)
XLA Ops:
  8.1 2.8 top_k.11
  14.2 1.9 broadcast_select_fusion.1
  17.2 1.3 compare_or_fusion
  20.1 1.3 and_select_fusion.5
  22.7 2.3 gather_fusion.4
  25.0 2.8 reshape.404
  27.8 1.9 gather_fusion.3
  30.1 2.3 gather_fusion
  32.5 2.2 gather.29
  34.7 4.1 fusion.16
  38.8 13.0 all-to-all-start
  54.6 10.6 all_gather.6
  66.1 10.1 all_gather.7
  77.4 562.3 %all-reduce.10.cloned.1.call-done = (bf16[3,2048,128]{2,1,0:T(8,128)(2,1)}, bf16[3,2048,128]{2,1,0:T(8,128)(2,1)}) async-done(((bf16[3,2048,128]{2,1,0:T(8,128)(2,1)}, bf16[3,2048,128]{2,1,0:T(8,128)(2,1)}), (bf16[3,2048,128]{2,1,0:T(8,128)(2,1)}, bf16[3,2048,128]{2,1,0:T(8,128)(2,1)})) %all-reduce.10.cloned.1.call-update) | async-done | bytes 3145744 | tf_op jit(solution)/shard_map/psum | solution.py:9
  639.7 1.4 fusion.22
  643.9 1.3 multiply_convert_fusion.5
  648.0 3.0 pad_maximum_fusion.1
  651.1 8.8 all-to-all-start.2
  659.9 2.2 reshape.393
  662.1 18.8 %all-to-all-done.2 = bf16[64,4,2048]{2,1,0:T(4,128)(2,1)} async-done(((bf16[64,4,2048]{2,1,0:T(4,128)(2,1)}), bf16[64,4,2048]{2,1,0:T(4,128)(2,1)}, u32[]{:S(2)}, u32[]{:S(2)}) %all-to-all-start.2) | async-done | bytes 1048608 | tf_op jit(solution)/shard_map/all_to_all | solution.py:121
  680.9 2.1 reshape.398
  683.0 2.8 fusion.14
  690.2 5.2 pad_maximum_fusion
  695.4 2.5 fusion.12
  697.9 1.7 fusion.3
  699.6 2.2 reshape.399
  701.9 26.0 %all-to-all-start.3 = ((bf16[64,4,2048]{2,1,0:T(4,128)(2,1)}), bf16[64,4,2048]{2,1,0:T(4,128)(2,1)}, u32[]{:S(2)}, u32[]{:S(2)}) async-start(bf16[64,4,2048]{2,1,0:T(4,128)(2,1)} %reshape.399), calls=%async_computation.3 | async-start | bytes 2097152 | tf_op jit(solution)/shard_map/all_to_all | solution.py:125
  733.5 2.1 convolution_bitcast_fusion.9
  735.5 2.1 convolution_bitcast_fusion.10
  737.6 1.3 fusion.21
  739.0 7.6 all-to-all-done.3
  746.6 8.5 all-to-all-start.1
  755.1 1.3 pad_maximum_fusion.3
  756.4 1.5 copy.64
  757.9 1.3 fusion.4
  759.9 1.5 copy.73
  761.4 63.2 %all-reduce.11 = (bf16[2,48,2048]{2,0,1:T(2,128)(2,1)}, bf16[2,48,2048]{2,0,1:T(2,128)(2,1)S(1)}) all-reduce(f32[2,48,2048]{2,0,1:T(2,128)} %copy.64, f32[2,48,2048]{2,0,1:T(2,128)} %copy.73), channel_id=2, replica_groups=mesh['expert'=64,'dp'=4] {'dp'}, use_global_device_ids=true, to_apply=%region_10.11.clone | all-reduce | flops 393216 | bytes 2359296
  825.8 2.1 reshape.400
  829.0 3.5 maximum_maximum_fusion.1
  832.5 4.8 gather_fusion.2
  837.2 3.4 reshape.403
  840.6 2.3 gather_fusion.7
  843.0 1.8 reshape.402
  844.7 3.6 reduce_sum.70
  848.4 6.3 multiply_reduce_fusion
  855.3 507.4 %all-reduce.8.cloned.1.call-done = f32[2,3,2048,128]{3,2,1,0:T(8,128)} async-done(((f32[2,3,2048,128]{3,2,1,0:T(8,128)}), f32[2,3,2048,128]{3,2,1,0:T(8,128)}) %all-reduce.8.cloned.1.call-update) | async-done | bytes 6291472 | tf_op jit(solution)/shard_map/psum | solution.py:187
  1362.7 5.4 fusion.2
  1368.1 1.7 fusion.37
  (134 shorter events, 29.5 us)
Async XLA Ops:
  8.0 4.8 copy-start
  8.0 631.7 %all-reduce.10.cloned.1.call-start = ((), (), s32[]{:S(2)}) async-start(), calls=%async_computation.7 | async-start | bytes 6291456 | tf_op jit(solution)/shard_map/psum | solution.py:9
  16.1 0.7 copy-start.17
  16.1 5.3 copy-start.19
  16.1 6.6 copy-start.1
  21.6 1.1 copy-start.10
  25.0 5.1 copy-start.2
  38.8 612.3 %all-to-all-start = ((bf16[64,4,2048]{2,1,0:T(4,128)(2,1)}), bf16[64,4,2048]{2,1,0:T(4,128)(2,1)}, u32[]{:S(2)}, u32[]{:S(2)}) async-start(bf16[64,4,2048]{2,1,0:T(4,128)(2,1)} %get-tuple-element.53), calls=%async_computation | async-start | bytes 2097152 | tf_op jit(solution)/shard_map/all_to_all | solution.py:110
  51.8 1310.9 %all-reduce.8.cloned.1.call-start = ((), (), s32[]{:S(2)}) async-start(), calls=%async_computation.6 | async-start | bytes 12582912 | tf_op jit(solution)/shard_map/psum | solution.py:187
  639.7 3.9 copy-start.5
  639.7 4.2 copy-start.9
  645.2 1.0 copy-start.16
  646.5 1.3 copy-start.12
  646.5 1.3 copy-start.14
  651.1 29.8 %all-to-all-start.2 = ((bf16[64,4,2048]{2,1,0:T(4,128)(2,1)}), bf16[64,4,2048]{2,1,0:T(4,128)(2,1)}, u32[]{:S(2)}, u32[]{:S(2)}) async-start(bf16[64,4,2048]{2,1,0:T(4,128)(2,1)} %get-tuple-element.52), calls=%async_computation.2 | async-start | bytes 2097152 | tf_op jit(solution)/shard_map/all_to_all | solution.py:121
  659.9 702.9 %reduce-scatter.2.cloned.1.call-start = ((), (), s32[]{:S(2)}) async-start(), calls=%async_computation.5 | async-start | bytes 15728640 | tf_op jit(solution)/shard_map/reduce_scatter | solution.py:190
  683.0 2.8 copy-start.3
  683.0 2.9 copy-start.7
  685.9 1.2 copy-start.4
  695.4 2.5 copy-start.8
  701.9 27.1 %copy-start.20 = (u32[256]{0:T(256)S(1)}, u32[256]{0:T(256)}, u32[]{:S(2)}) copy-start(u32[256]{0:T(256)} %constant.84) | copy-start | bytes 3076
  701.9 44.7 %all-to-all-start.3 = ((bf16[64,4,2048]{2,1,0:T(4,128)(2,1)}), bf16[64,4,2048]{2,1,0:T(4,128)(2,1)}, u32[]{:S(2)}, u32[]{:S(2)}) async-start(bf16[64,4,2048]{2,1,0:T(4,128)(2,1)} %reshape.399), calls=%async_computation.3 | async-start | bytes 2097152 | tf_op jit(solution)/shard_map/all_to_all | solution.py:125
  746.6 81.3 %all-to-all-start.1 = ((bf16[64,4,2048]{2,1,0:T(4,128)(2,1)}), bf16[64,4,2048]{2,1,0:T(4,128)(2,1)S(1)}, u32[]{:S(2)}, u32[]{:S(2)}) async-start(bf16[64,4,2048]{2,1,0:T(4,128)(2,1)} %reshape.394), calls=%async_computation.1 | async-start | bytes 2097152 | tf_op jit(solution)/shard_map/all_to_all | solution.py:114
  755.1 4.2 copy-start.6
  755.1 4.2 copy-start.15
  756.4 3.1 copy-start.13
  825.8 3.2 copy-start.18
  843.0 5.4 copy-start.11
Sparse Core Ops, SparseCore 0:
  16.3 623.4 all-reduce.9
  651.2 711.4 all-reduce.7
Sparse Core Ops, SparseCore 1:
  695.5 151.1 reduce-scatter.1
where the time goes:
time: 1390 us; the launch traced here: 1380 us
  waiting for transfers between devices  1100 us (79%)
  blocking collectives  83.8 us (6%)
  starting transfers between devices  56.4 us (4%)
  local copies, waits for them, and re-layouts  52.8 us (4%)
  other arithmetic  43.3 us (3%)
  matrix products  26.6 us (2%)
  between operations  18.3 us (1%)
    psum x1, waiting for transfers between devices, spread(): return lax.psum(jnp.where(mine, array, jnp.zeros_like(array)), axis)  562 us
    psum x1, waiting for transfers between devices, per_device(): summed = lax.psum(shadow, 'expert')  507 us
    unnamed x1, blocking collectives  63.2 us
  transfers between devices with their start and end apart: 7, of which 4 were waited for; matrix products, arithmetic and copies ran while one was open for 8% of the time, Pallas kernels for 0%

commit v1 on v0

v1 whole, which is shorter than its diff:
```python
import functools

import jax
import jax.numpy as jnp
from jax import lax
from jax.experimental import pallas as pl
from jax.experimental.pallas import tpu as pltpu
from jax.sharding import Mesh
from jax.sharding import PartitionSpec as P

D = 2048
H = 512
TOK = 128
EXPERTS = 64
CAP = 4
HOT_CAP = 12
SLOT = 2 * CAP
SENT = EXPERTS * SLOT
PAIR = 2 * HOT_CAP
SHARE = 128
WROWS = 3 * D
NZ, NXL, NY, NXH, NC = 8, 2, 4, 2, 2
ALL = ("z", "xl", "y", "xh", "c")
E = ("z", "xl", "y")
X = ("xh", "xl")
BF = jnp.bfloat16
F32 = jnp.float32
MIB = 1024 * 1024


def contract(a, b, da, db):
    return lax.dot_general(a, b, (((da,), (db,)), ((), ())), preferred_element_type=F32)


def iota(shape, dim):
    return lax.broadcasted_iota(jnp.int32, shape, dim)


def cost(flops, nbytes):
    return pl.CostEstimate(flops=int(flops), bytes_accessed=int(nbytes), transcendentals=0)


def whole(space=pltpu.VMEM):
    return pl.BlockSpec(memory_space=space)


def pack_kernel(core_ref, counts_ref, routes_ref, combine_ref, tokens_ref, cot_ref,
                send_ref, mine_ref, theirs_ref, slots_ref):
    core = core_ref[0]
    counts = counts_ref[...].astype(F32)
    ids = iota((1, EXPERTS), 1).astype(F32)
    low = jnp.float32(-3.0e38)

    def largest(values):
        top = jnp.max(values, axis=1, keepdims=True)
        return jnp.min(jnp.where(values == top, ids, float(EXPERTS)), axis=1, keepdims=True)

    hot0 = largest(counts)
    hot1 = largest(jnp.where(ids == hot0, low, counts))
    eid = iota((EXPERTS, TOK), 0)
    routes = [routes_ref[k:k + 1, :] for k in range(2)]
    weight = [combine_ref[k:k + 1, :] for k in range(2)]
    oh = [(eid == r).astype(F32) for r in routes]
    earlier = (iota((TOK, TOK), 0) < iota((TOK, TOK), 1)).astype(F32).astype(BF)
    cum = jnp.dot((oh[0] + oh[1]).astype(BF), earlier, preferred_element_type=F32)
    rank = [jnp.sum(cum * oh[0], axis=0, keepdims=True),
            jnp.sum((cum + oh[0]) * oh[1], axis=0, keepdims=True)]
    main, mine, theirs = [], [], []
    for k in range(2):
        rf = routes[k].astype(F32)
        lead = rf == hot0
        hot = lead | (rf == hot1)
        member = jnp.where(lead, 0, 1)
        r = rank[k].astype(jnp.int32)
        keep = r < jnp.where(hot, HOT_CAP, CAP)
        main.append(jnp.where(keep & jnp.logical_not(hot), routes[k] * SLOT + r, -1))
        mine.append(jnp.where(keep & hot & (member == core), r, -1))
        theirs.append(jnp.where(keep & hot & (member != core), r, -1))
        slots_ref[k:k + 1, :] = jnp.where(
            main[k] >= 0, main[k],
            jnp.where(mine[k] >= 0, SENT + mine[k], jnp.where(theirs[k] >= 0, SENT + PAIR + theirs[k], -1)))

    def rows(slot, shift, base, count):
        sid = iota((count, TOK), 0) + base
        at = [jnp.where(s >= 0, s + shift, -1) for s in slot]
        hit = [sid == s for s in slot]
        hit_c = [sid == a for a in at]
        pick = (hit[0] | hit[1]).astype(F32).astype(BF)
        pick_c = (hit_c[0] | hit_c[1]).astype(F32).astype(BF)
        w = jnp.sum(jnp.where(hit_c[0], weight[0], 0.0) + jnp.where(hit_c[1], weight[1], 0.0),
                    axis=1, keepdims=True)
        data = jnp.dot(pick, tokens_ref[...], preferred_element_type=F32)
        cot = jnp.dot(pick_c, cot_ref[...], preferred_element_type=F32)
        return (data + w * cot).astype(BF)

    mine_ref[...] = rows(mine, HOT_CAP, 0, PAIR)
    theirs_ref[...] = rows(theirs, HOT_CAP, 0, PAIR)
    step = 128

    def body(i, carry):
        base = pl.multiple_of(i * step, step)
        send_ref[pl.ds(base, step), :] = rows(main, CAP, base, step)
        return carry

    lax.fori_loop(0, SENT // step, body, 0)


def pack(core, counts, routes_t, combine_t, tokens, cotangent):
    return pl.pallas_call(
        pack_kernel,
        out_shape=(jax.ShapeDtypeStruct((SENT, D), BF), jax.ShapeDtypeStruct((PAIR, D), BF),
                   jax.ShapeDtypeStruct((PAIR, D), BF), jax.ShapeDtypeStruct((2, TOK), jnp.int32)),
        in_specs=[whole(pltpu.SMEM)] + [whole()] * 5,
        out_specs=(whole(),) * 4,
        compiler_params=pltpu.CompilerParams(vmem_limit_bytes=32 * MIB),
        cost_estimate=cost(4 * SENT * TOK * D, 4 * SENT * D),
        name="pack",
    )(core, counts, routes_t, combine_t, tokens, cotangent)


def backward_parts(gate, up, back):
    s = jax.nn.sigmoid(gate)
    act = (gate * s * up).astype(BF)
    gate_part = (back * up * s * (1.0 + gate * (1.0 - s))).astype(BF)
    up_part = (back * gate * s).astype(BF)
    return gate_part, up_part, act


def expert_kernel(got_ref, gate_ref, up_ref, down_ref, back_ref, data_ref, cot_ref, parts_ref):
    count = EXPERTS * CAP
    i, j = iota((count, SENT), 0), iota((count, SENT), 1)
    at = (i >> 2) * SLOT + (i & 3)
    data_ref[...] = jnp.dot((j == at).astype(F32).astype(BF), got_ref[...], preferred_element_type=F32).astype(BF)
    cot_ref[...] = jnp.dot((j == at + CAP).astype(F32).astype(BF), got_ref[...], preferred_element_type=F32).astype(BF)
    data, cot = data_ref[...], cot_ref[...]
    gate = jnp.dot(data, gate_ref[0], preferred_element_type=F32)
    up = jnp.dot(data, up_ref[0], preferred_element_type=F32)
    back = jnp.dot(cot, down_ref[0], preferred_element_type=F32)
    gate_part, up_part, act = backward_parts(gate, up, back)
    for m, part in enumerate((gate_part, up_part, act)):
        for q in range(H // SHARE):
            parts_ref[m, q] = part[:, q * SHARE:(q + 1) * SHARE]
    out = contract(act, down_ref[0], 1, 1).astype(BF)
    inp = (contract(gate_part, gate_ref[0], 1, 1) + contract(up_part, up_ref[0], 1, 1)).astype(BF)
    i, j = iota((SENT, count), 1), iota((SENT, count), 0)
    at = (i >> 2) * SLOT + (i & 3)
    back_ref[...] = (jnp.dot((j == at).astype(F32).astype(BF), out, preferred_element_type=F32)
                     + jnp.dot((j == at + CAP).astype(F32).astype(BF), inp, preferred_element_type=F32)).astype(BF)


def run_expert(got, gate_weight, up_weight, down_weight):
    count = EXPERTS * CAP
    return pl.pallas_call(
        expert_kernel,
        out_shape=(jax.ShapeDtypeStruct((SENT, D), BF), jax.ShapeDtypeStruct((count, D), BF),
                   jax.ShapeDtypeStruct((count, D), BF),
                   jax.ShapeDtypeStruct((3, H // SHARE, count, SHARE), BF)),
        in_specs=[whole()] * 4,
        out_specs=(whole(),) * 4,
        compiler_params=pltpu.CompilerParams(vmem_limit_bytes=48 * MIB),
        cost_estimate=cost(12 * count * D * H + 8 * SENT * count * D, 12 * MIB),
        name="expert",
    )(got, gate_weight, up_weight, down_weight)


def grads_kernel(core_ref, data_ref, cot_ref, parts_ref, keep_ref, send_ref):
    core = core_ref[0]
    order = (core, 2 + core, 1 - core, 3 - core)
    pick = [[parts_ref[m, q] for q in order] for m in range(3)]
    first = contract(data_ref[...], jnp.concatenate(pick[0] + pick[1], axis=1), 0, 0)
    second = contract(cot_ref[...], jnp.concatenate(pick[2], axis=1), 0, 0)
    for m in range(3):
        for n in range(4):
            at = ((m * 4 + n) if m < 2 else n) * SHARE
            value = (first if m < 2 else second)[:, at:at + SHARE]
            if n < 2:
                keep_ref[n, m] = value
            else:
                send_ref[n - 2, m] = value.astype(BF)


def main_grads(core, data, cot, parts):
    count = EXPERTS * CAP
    block = 512
    return pl.pallas_call(
        grads_kernel,
        grid=(D // block,),
        out_shape=(jax.ShapeDtypeStruct((2, 3, D, SHARE), F32), jax.ShapeDtypeStruct((2, 3, D, SHARE), BF)),
        in_specs=[whole(pltpu.SMEM),
                  pl.BlockSpec((count, block), lambda i: (0, i)),
                  pl.BlockSpec((count, block), lambda i: (0, i)),
                  pl.BlockSpec((3, H // SHARE, count, SHARE), lambda i: (0, 0, 0, 0))],
        out_specs=(pl.BlockSpec((2, 3, block, SHARE), lambda i: (0, 0, i, 0)),
                   pl.BlockSpec((2, 3, block, SHARE), lambda i: (0, 0, i, 0))),
        compiler_params=pltpu.CompilerParams(vmem_limit_bytes=40 * MIB),
        cost_estimate=cost(6 * count * D * H, 12 * MIB),
        name="main_grads",
    )(core, data, cot, parts)


def hot_kernel(rows_ref, weights_ref, ret_ref, grads_ref):
    total = NXH * NXL * 2 * PAIR
    count = total // 2

    def place(i):
        group = jnp.floor((i.astype(F32) + 0.5) * (1.0 / HOT_CAP)).astype(jnp.int32)
        return group * HOT_CAP + i

    i, j = iota((count, total), 0), iota((count, total), 1)
    at = place(i)
    data = jnp.dot((j == at).astype(F32).astype(BF), rows_ref[...], preferred_element_type=F32).astype(BF)
    cot = jnp.dot((j == at + HOT_CAP).astype(F32).astype(BF), rows_ref[...], preferred_element_type=F32).astype(BF)
    gate_w, up_w, down_w = (weights_ref[m * D:(m + 1) * D, :] for m in range(3))
    gate = jnp.dot(data, gate_w, preferred_element_type=F32)
    up = jnp.dot(data, up_w, preferred_element_type=F32)
    back = jnp.dot(cot, down_w, preferred_element_type=F32)
    gate_part, up_part, act = backward_parts(gate, up, back)
    out = contract(act, down_w, 1, 1).astype(BF)
    inp = (contract(gate_part, gate_w, 1, 1) + contract(up_part, up_w, 1, 1)).astype(BF)
    i, j = iota((total, count), 1), iota((total, count), 0)
    at = place(i)
    ret_ref[...] = (jnp.dot((j == at).astype(F32).astype(BF), out, preferred_element_type=F32)
                    + jnp.dot((j == at + HOT_CAP).astype(F32).astype(BF), inp, preferred_element_type=F32)).astype(BF)
    grads_ref[0:D, :] = contract(data, gate_part, 0, 0).astype(BF)
    grads_ref[D:2 * D, :] = contract(data, up_part, 0, 0).astype(BF)
    grads_ref[2 * D:3 * D, :] = contract(cot, act, 0, 0).astype(BF)


def run_hot(rows, weights):
    return pl.pallas_call(
        hot_kernel,
        out_shape=(jax.ShapeDtypeStruct(rows.shape, BF), jax.ShapeDtypeStruct((WROWS, SHARE), BF)),
        in_specs=[whole()] * 2,
        out_specs=(whole(),) * 2,
        compiler_params=pltpu.CompilerParams(vmem_limit_bytes=40 * MIB),
        cost_estimate=cost(18 * 96 * D * SHARE, 5 * MIB),
        name="hot",
    )(rows, weights)


def combine_kernel(back_ref, mine_ref, theirs_ref, slots_ref, combine_ref, cot_ref,
                   mixed_ref, input_ref, cgrad_ref):
    slot = [slots_ref[:, k:k + 1] for k in range(2)]

    def pick(base, count, shift):
        lane = iota((TOK, count), 1) + (base - shift)
        inside = iota((TOK, count), 1) >= shift
        return [jnp.where((lane == s) & (s >= base) & inside, 1.0, 0.0) for s in slot]

    tables = ((back_ref, 0, SENT, CAP), (mine_ref, SENT, PAIR, HOT_CAP), (theirs_ref, SENT + PAIR, PAIR, HOT_CAP))
    outs = []
    for k in range(2):
        total = None
        for ref, base, count, shift in tables:
            term = jnp.dot(pick(base, count, 0)[k].astype(BF), ref[...], preferred_element_type=F32)
            total = term if total is None else total + term
        outs.append(total)
    total = None
    for ref, base, count, shift in tables:
        both = pick(base, count, shift)
        term = jnp.dot((both[0] + both[1]).astype(BF), ref[...], preferred_element_type=F32)
        total = term if total is None else total + term
    input_ref[...] = total.astype(BF)
    mixed_ref[...] = (combine_ref[:, 0:1] * outs[0] + combine_ref[:, 1:2] * outs[1]).astype(BF)
    cot = cot_ref[...].astype(F32)
    for k in range(2):
        cgrad_ref[:, k:k + 1] = jnp.sum(outs[k] * cot, axis=1, keepdims=True)


def combine_rows(back, mine, theirs, slots, combine, cotangent):
    return pl.pallas_call(
        combine_kernel,
        out_shape=(jax.ShapeDtypeStruct((TOK, D), BF), jax.ShapeDtypeStruct((TOK, D), BF),
                   jax.ShapeDtypeStruct((TOK, 2), F32)),
        in_specs=[whole()] * 6,
        out_specs=(whole(),) * 3,
        compiler_params=pltpu.CompilerParams(vmem_limit_bytes=32 * MIB),
        cost_estimate=cost(6 * TOK * SENT * D, 4 * MIB),
        name="combine",
    )(back, mine, theirs, slots, combine, cotangent)


def exchange(x, axes):
    return lax.all_to_all(x, axes, split_axis=0, concat_axis=0, tiled=True)


def swap(x, axis):
    return lax.ppermute(x, axis, [(0, 1), (1, 0)])


def in_core_order(own, other, core):
    first = core == 0
    return jnp.where(first, own, other), jnp.where(first, other, own)


def hot_weights(gate_weight, up_weight, down_weight, roots, core, xh):
    stacked = [
        jnp.concatenate([lax.dynamic_slice_in_dim(w[0], (2 * xh + xl) * SHARE, SHARE, 1)
                         for w in (gate_weight, up_weight, down_weight)], axis=0)
        .reshape(NZ, NY, 2, WROWS // 64, SHARE)
        for xl in range(NXL)
    ]
    halves = [lax.dynamic_index_in_dim(s, core, 2, keepdims=False) for s in stacked]
    sent = jnp.stack(halves, axis=1).reshape(WROWS, SHARE)
    got = exchange(sent, E).reshape(EXPERTS, WROWS // 64, SHARE)
    own = lax.dynamic_index_in_dim(got, jnp.where(core == 0, roots[0], roots[1]), 0, keepdims=False)
    other = lax.dynamic_index_in_dim(got, jnp.where(core == 0, roots[1], roots[0]), 0, keepdims=False)
    first, second = in_core_order(own, swap(other, "c"), core)
    piece = jnp.concatenate([first, second], axis=0)
    piece = lax.all_gather(piece, "y", axis=0, tiled=True)
    return lax.all_gather(piece, "z", axis=0, tiled=True)


def reduce_over(x, axis, size):
    parts = exchange(x, axis).reshape(size, -1, SHARE)
    return jnp.sum(parts.astype(F32), axis=0)


def hot_grads_home(grads, roots, core):
    part = reduce_over(grads, "y", NY).astype(BF)
    part = reduce_over(part, "z", NZ).astype(BF).reshape(2, WROWS // 64, SHARE)
    own = lax.dynamic_index_in_dim(part, core, 0, keepdims=False)
    other = swap(lax.dynamic_index_in_dim(part, 1 - core, 0, keepdims=False), "c")
    dest = iota((EXPERTS, 1, 1), 0)
    mine = jnp.where(core == 0, roots[0], roots[1])
    theirs = jnp.where(core == 0, roots[1], roots[0])
    zero = jnp.zeros((), BF)
    sent = jnp.where(dest == mine, own[None], jnp.where(dest == theirs, other[None], zero))
    got = exchange(sent.reshape(WROWS, SHARE), E).reshape(NZ, NXL, NY, WROWS // 64, SHARE)
    keep = lax.dynamic_index_in_dim(got, core, 1, keepdims=False)
    give = swap(lax.dynamic_index_in_dim(got, 1 - core, 1, keepdims=False), "c")
    first, second = in_core_order(keep, give, core)
    both = jnp.stack([first, second], axis=2)
    return jnp.transpose(both, (1, 0, 2, 3, 4)).reshape(3, D, SHARE).astype(F32)


def per_device(tokens, cotangent, routes, combine, counts, gate_weight, up_weight, down_weight):
    core = lax.axis_index("c")
    xh = lax.axis_index("xh")
    core_arg = core.astype(jnp.int32).reshape(1)
    ids = jnp.arange(EXPERTS, dtype=jnp.int32)
    root0 = jnp.argmax(counts).astype(jnp.int32)
    root1 = jnp.argmax(jnp.where(ids == root0, jnp.iinfo(jnp.int32).min, counts)).astype(jnp.int32)
    roots = (root0, root1)

    weights = hot_weights(gate_weight, up_weight, down_weight, roots, core, xh)
    send, mine, theirs, slots = pack(core_arg, counts.reshape(1, EXPERTS), routes.T, combine.T, tokens, cotangent)
    got = exchange(send, E)
    hot_rows = jnp.concatenate([mine, swap(theirs, "c")], axis=0)
    hot_rows = lax.all_gather(hot_rows, X, axis=0, tiled=True)

    back, data, cot, parts = run_expert(got, gate_weight, up_weight, down_weight)
    back = exchange(back, E)

    ret, shadow = run_hot(hot_rows, weights)
    ret = exchange(ret, X).reshape(NXH * NXL, 2, PAIR, D)
    ret = jnp.sum(ret.astype(F32), axis=0).astype(BF)
    hot_mine = ret[0]
    hot_theirs = swap(ret[1], "c")

    keep, give = main_grads(core_arg, data, cot, parts)
    half = keep + swap(give, "c").astype(F32)
    part = lax.dynamic_index_in_dim(half, xh, 0, keepdims=False)
    other = swap(lax.dynamic_index_in_dim(half, 1 - xh, 0, keepdims=False).astype(BF), "xh")

    shadow = hot_grads_home(shadow, roots, core)
    grads = part + other.astype(F32) + shadow

    mixed, input_grad, combine_grad = combine_rows(back, hot_mine, hot_theirs, slots.T, combine, cotangent)
    return mixed, input_grad, combine_grad, grads[0][None], grads[1][None], grads[2][None]


def solution(mesh):
    split = Mesh(mesh.devices.reshape(NZ, NXL, NY, NXH, NC), ALL)
    rows = P(ALL, None)
    owned = P(E, None, None)
    grads = P(E, None, ("xh", "c"))
    return jax.shard_map(
        per_device,
        mesh=split,
        in_specs=(rows, rows, rows, rows, P(), owned, owned, owned),
        out_specs=(rows, rows, rows, grads, grads, grads),
        check_vma=False,
    )
```

time: 1390 us -> 337 us (0.24)
  waiting for transfers between devices: 1100 us -> 161 us
  local copies, waits for them, and re-layouts: 52.8 us -> 17.7 us
  other arithmetic: 43.3 us -> 14.1 us
  matrix products: 26.6 us -> 0 us
  Pallas kernels: 0 us -> 23.8 us
  blocking collectives: 83.8 us -> 61.7 us
  starting transfers between devices: 56.4 us -> 39.5 us
    psum x2 -> x0, waiting for transfers between devices: 1070 us -> none  [the longest x1 562 us: spread(): return lax.psum(jnp.where(mine, array, jnp.zeros_like(array)), axis)]
    all_to_all x4 -> x5, waiting for transfers between devices: 26.4 us -> 134 us  [exchange(): return lax.all_to_all(x, axes, split_axis=0, concat_axis=0, tiled=True)]
    unnamed x1 -> x0, blocking collectives: 63.2 us -> none
    all_to_all x0 -> x2, blocking collectives: none -> 36.1 us  [exchange(): return lax.all_to_all(x, axes, split_axis=0, concat_axis=0, tiled=True)]
    dot_general x27 -> x0, matrix products: 26.6 us -> none  [the longest x3 5.42 us: expert_forward(): jnp.dot(row_data, gate_weight, preferred_element_type=jnp.float32)]
    pallas_call x0 -> x5, Pallas kernels: none -> 23.8 us  [the longest x1 10.6 us: run_expert(): pl.pallas_call(expert_kernel, out_shape=(jax.ShapeDtypeStruct((SENT, D),...]
    all_gather x0 -> x1, waiting for transfers between devices: none -> 19 us  [hot_weights(): return lax.all_gather(piece, 'z', axis=0, tiled=True)]
    all_to_all x4 -> x5, starting transfers between devices: 56.3 us -> 37.7 us  [exchange(): return lax.all_to_all(x, axes, split_axis=0, concat_axis=0, tiled=True)]
  transfers between devices with their start and end apart: 7 -> 13, of which waited for: 4 -> 10; matrix products, arithmetic and copies ran while one was open for 8% -> 5% of each run, Pallas kernels for 0% -> 6%
where the time goes in v1:
time: 337 us; the launch traced here: 335 us
  waiting for transfers between devices  161 us (48%)
  blocking collectives  61.7 us (18%)
  starting transfers between devices  39.5 us (12%)
  Pallas kernels  23.8 us (7%)
  local copies, waits for them, and re-layouts  17.7 us (5%)
  between operations  16.9 us (5%)
  other arithmetic  14.1 us (4%)
    all_to_all x5, waiting for transfers between devices, exchange(): return lax.all_to_all(x, axes, split_axis=0, concat_axis=0, tiled=True)  134 us
    all_to_all x5, starting transfers between devices, exchange(): return lax.all_to_all(x, axes, split_axis=0, concat_axis=0, tiled=True)  37.7 us
    all_to_all x2, blocking collectives, exchange(): return lax.all_to_all(x, axes, split_axis=0, concat_axis=0, tiled=True)  36.1 us
    all_gather x1, waiting for transfers between devices, hot_weights(): return lax.all_gather(piece, 'z', axis=0, tiled=True)  19 us
    all_gather x1, blocking collectives, hot_weights(): piece = lax.all_gather(piece, 'y', axis=0, tiled=True)  13.2 us
    all_gather x1, blocking collectives, per_device(): hot_rows = lax.all_gather(hot_rows, X, axis=0, tiled=True)  12.4 us
    pallas_call x1, Pallas kernels, run_expert(): pl.pallas_call(expert_kernel, out_shape=(jax.ShapeDtypeStruct((SENT, D),...  10.6 us
    unnamed x28, local copies, waits for them, and re-layouts  9.17 us
  transfers between devices with their start and end apart: 13, of which 10 were waited for; matrix products, arithmetic and copies ran while one was open for 5% of the time, Pallas kernels for 6%

profile of v1, /device:TPU:4, one launch (start us, length us, event | category | flops | bytes accessed | tf_op | source)
XLA Modules:
  0.0 334.7 jit_solution(15528383586106318746)
XLA Ops:
  7.2 1.4 dynamic-slice_bitcast_fusion.8
  8.6 0.5 copy-done.10
  9.1 1.5 dynamic-slice_bitcast_fusion.6
  11.0 1.3 pad_maximum_fusion.2
  12.3 12.9 %all-to-all-start.2 = ((bf16[64,96,128]{2,1,0:T(8,128)(2,1)}), bf16[64,96,128]{2,1,0:T(8,128)(2,1)S(1)}, u32[]{:S(2)}, u32[]{:S(2)}) async-start(bf16[64,96,128]{2,1,0:T(8,128)(2,1)} %bitcast.18), calls=%async_computation.2 | async-start | bytes 3145728 | tf_op jit(solution)/shard_map/all_to_all | solution.py:284
  25.3 0.7 iota_reduce_fusion
  25.9 1.3 fusion.4
  28.5 35.9 %all-to-all-done.2 = bf16[64,96,128]{2,1,0:T(8,128)(2,1)S(1)} async-done(((bf16[64,96,128]{2,1,0:T(8,128)(2,1)}), bf16[64,96,128]{2,1,0:T(8,128)(2,1)S(1)}, u32[]{:S(2)}, u32[]{:S(2)}) %all-to-all-start.2) | async-done | bytes 1572896 | tf_op jit(solution)/shard_map/all_to_all | solution.py:284
  65.8 13.2 %all_gather.10 = bf16[768,128]{1,0:T(8,128)(2,1)} all-gather(bf16[192,128]{1,0:T(8,128)(2,1)S(1)} %pad_maximum_fusion.4), channel_id=1, replica_groups=mesh['z'=8,'xl'=2,'y'=4,'xh'=2,'c'=2] {'y'}, dimensions={0}, use_global_device_ids=true | all-gather | bytes 245760 | tf_op jit(solution)/shard_map/all_gather | solution.py:310
  79.1 3.8 %pack.1 = (bf16[512,2048]{1,0:T(8,128)(2,1)}, bf16[24,2048]{1,0:T(8,128)(2,1)S(1)}, bf16[24,2048]{1,0:T(8,128)(2,1)S(1)}, s32[2,128]{1,0:T(2,128)S(1)}) custom-call(s32[1]{0:T(128)} %bitcast.core_ref, s32[1,64]{1,0:T(1,128)S(1)} %bitcast.68, s32[2,128]{1,0:T(2,128)S(1)} %bitcast.69, f32[2,128]{1,0:T(2,128)S(1)} %bitcast.67, bf16[128,2048]{1,0:T(8,128)(2,1)S(1)} %copy-done.4, ...), custom_call_target="tpu_custom_call" | custom-call | flops 536870912 | bytes 4194304 | tf_op jit(solution)/shard_map/pack/pallas_call | solution.py:109
  82.8 1.3 collective-permute-done
  84.1 12.4 %all_gather.9.rows_ref = bf16[192,2048]{1,0:T(8,128)(2,1)S(1)} all-gather(bf16[48,2048]{1,0:T(8,128)(2,1)S(1)} %pad_maximum_fusion.3), channel_id=1, replica_groups=mesh['z'=8,'xl'=2,'y'=4,'xh'=2,'c'=2] {'xh','xl'}, dimensions={0}, use_global_device_ids=true | all-gather | bytes 983040 | tf_op jit(solution)/shard_map/all_gather | solution.py:350
  96.6 19.0 %all-gather.2.cloned.1.call-done.weights_ref = bf16[6144,128]{1,0:T(8,128)(2,1)} async-done(((bf16[768,128]{1,0:T(8,128)(2,1)}), bf16[6144,128]{1,0:T(8,128)(2,1)}) %all-gather.2.cloned.1.call-update) | async-done | bytes 1572880 | tf_op jit(solution)/shard_map/all_gather | solution.py:311
  115.5 1.4 copy-done.1
  117.0 2.6 hot.1
  119.5 20.8 %all_to_all.64 = bf16[4,1536,128]{2,1,0:T(8,128)(2,1)S(1)} all-to-all(bf16[4,1536,128]{2,1,0:T(8,128)(2,1)S(1)} %bitcast.65), channel_id=1, replica_groups=mesh['z'=8,'xl'=2,'y'=4,'xh'=2,'c'=2] {'y'}, dimensions={0} | all-to-all | bytes 3145728 | tf_op jit(solution)/shard_map/all_to_all | solution.py:284
  140.3 6.6 %all-to-all-start = ((bf16[64,8,2048]{2,1,0:T(8,128)(2,1)}), bf16[64,8,2048]{2,1,0:T(8,128)(2,1)}, u32[]{:S(2)}, u32[]{:S(2)}) async-start(bf16[64,8,2048]{2,1,0:T(8,128)(2,1)} %bitcast.4), calls=%async_computation | async-start | bytes 4194304 | tf_op jit(solution)/shard_map/all_to_all | solution.py:284
  146.8 0.5 reduce_sum.37
  147.3 44.2 %all-to-all-done = bf16[64,8,2048]{2,1,0:T(8,128)(2,1)} async-done(((bf16[64,8,2048]{2,1,0:T(8,128)(2,1)}), bf16[64,8,2048]{2,1,0:T(8,128)(2,1)}, u32[]{:S(2)}, u32[]{:S(2)}) %all-to-all-start) | async-done | bytes 2097184 | tf_op jit(solution)/shard_map/all_to_all | solution.py:284
  191.5 15.3 %all_to_all.65 = bf16[8,192,128]{2,1,0:T(8,128)(2,1)S(1)} all-to-all(bf16[8,192,128]{2,1,0:T(8,128)(2,1)S(1)} %bitcast.77), channel_id=1, replica_groups=mesh['z'=8,'xl'=2,'y'=4,'xh'=2,'c'=2] {'z'}, dimensions={0} | all-to-all | bytes 786432 | tf_op jit(solution)/shard_map/all_to_all | solution.py:284
  206.9 5.0 %all-to-all-start.3 = ((bf16[4,48,2048]{2,1,0:T(8,128)(2,1)}), bf16[4,48,2048]{2,1,0:T(8,128)(2,1)S(1)}, u32[]{:S(2)}, u32[]{:S(2)}) async-start(bf16[4,48,2048]{2,1,0:T(8,128)(2,1)} %bitcast.21), calls=%async_computation.3 | async-start | bytes 1572864 | tf_op jit(solution)/shard_map/all_to_all | solution.py:284
  212.0 1.2 collective-permute-done.5
  213.2 1.4 select_select_fusion
  214.6 3.7 %all-to-all-done.3 = bf16[4,48,2048]{2,1,0:T(8,128)(2,1)S(1)} async-done(((bf16[4,48,2048]{2,1,0:T(8,128)(2,1)}), bf16[4,48,2048]{2,1,0:T(8,128)(2,1)S(1)}, u32[]{:S(2)}, u32[]{:S(2)}) %all-to-all-start.3) | async-done | bytes 786464 | tf_op jit(solution)/shard_map/all_to_all | solution.py:284
  218.4 6.5 %all-to-all-start.6 = ((bf16[64,96,128]{2,1,0:T(8,128)(2,1)}), bf16[64,96,128]{2,1,0:T(8,128)(2,1)S(1)}, u32[]{:S(2)}, u32[]{:S(2)}) async-start(bf16[64,96,128]{2,1,0:T(8,128)(2,1)} %select_select_fusion), calls=%async_computation.6 | async-start | bytes 3145728 | tf_op jit(solution)/shard_map/all_to_all | solution.py:284
  224.9 10.6 %expert.1 = (bf16[512,2048]{1,0:T(8,128)(2,1)}, bf16[256,2048]{1,0:T(8,128)(2,1)S(1)}, bf16[256,2048]{1,0:T(8,128)(2,1)S(1)}, bf16[3,4,256,128]{3,2,1,0:T(8,128)(2,1)S(1)}) custom-call(bf16[512,2048]{1,0:T(8,128)(2,1)} %bitcast.5.got_ref, bf16[1,2048,512]{2,1,0:T(8,128)(2,1)} %gate_ref.1, bf16[1,2048,512]{2,1,0:T(8,128)(2,1)} %up_ref.1, ...), custom_call_target="tpu_custom_call" | custom-call | flops 5368709120 | bytes 12582912 | tf_op jit(solution)/shard_map/expert/pallas_call | solution.py:153
  235.4 4.1 %main_grads.1 = (f32[2,3,2048,128]{3,2,1,0:T(8,128)S(1)}, bf16[2,3,2048,128]{3,2,1,0:T(8,128)(2,1)}) custom-call(s32[1]{0:T(128)} %bitcast.core_ref, bf16[256,2048]{1,0:T(8,128)(2,1)S(1)} %get-tuple-element.34.data_ref, bf16[256,2048]{1,0:T(8,128)(2,1)S(1)} %get-tuple-element.35.cot_ref, bf16[3,4,256,128]{3,2,1,0:T(8,128)(2,1)S(1)} %get-tuple-element.36.parts_ref), custom_call_target="tpu_custom_call" | custom-call | flops 1610612736 | bytes 12582912 | tf_op jit(solution)/shard_map/main_grads/pallas_call | solution.py:185
  239.5 2.7 copy-done
  242.2 17.4 %all-to-all-done.6 = bf16[64,96,128]{2,1,0:T(8,128)(2,1)S(1)} async-done(((bf16[64,96,128]{2,1,0:T(8,128)(2,1)}), bf16[64,96,128]{2,1,0:T(8,128)(2,1)S(1)}, u32[]{:S(2)}, u32[]{:S(2)}) %all-to-all-start.6) | async-done | bytes 1572896 | tf_op jit(solution)/shard_map/all_to_all | solution.py:284
  259.6 1.2 copy-done.8
  260.7 6.8 %all-to-all-start.1 = ((bf16[64,8,2048]{2,1,0:T(8,128)(2,1)}), bf16[64,8,2048]{2,1,0:T(8,128)(2,1)S(1)}, u32[]{:S(2)}, u32[]{:S(2)}) async-start(bf16[64,8,2048]{2,1,0:T(8,128)(2,1)} %bitcast.6), calls=%async_computation.1 | async-start | bytes 4194304 | tf_op jit(solution)/shard_map/all_to_all | solution.py:284
  267.6 4.2 %convert_add_fusion = f32[2,3,2048,128]{3,2,1,0:T(8,128)S(1)} fusion(f32[2,3,2048,128]{3,2,1,0:T(8,128)} %copy-done, bf16[2,3,2048,128]{3,2,1,0:T(8,128)(2,1)} %collective-permute-done.3), kind=kLoop, calls=%fused_computation | loop fusion | flops 3145728 | bytes 15728640 | tf_op jit(solution)/shard_map/add | solution.py:362
  271.8 2.7 copy-done.7
  274.5 1.4 fusion.1
  275.9 0.9 collective-permute-start.4
  276.7 0.9 dynamic-slice_bitcast_fusion
  277.7 0.8 reduce_sum.36
  278.5 1.0 fusion.6
  279.5 0.8 collective-permute-start.2
  280.5 0.7 collective-permute-done.2.theirs_ref
  281.2 32.4 %all-to-all-done.1 = bf16[64,8,2048]{2,1,0:T(8,128)(2,1)S(1)} async-done(((bf16[64,8,2048]{2,1,0:T(8,128)(2,1)}), bf16[64,8,2048]{2,1,0:T(8,128)(2,1)S(1)}, u32[]{:S(2)}, u32[]{:S(2)}) %all-to-all-start.1) | async-done | bytes 2097184 | tf_op jit(solution)/shard_map/all_to_all | solution.py:284
  313.6 2.8 combine.1
  316.4 0.6 copy.29
  317.1 1.6 fusion.2
  318.9 0.3 copy.28
  319.2 5.1 %collective-permute-done.4 = bf16[3,2048,128]{2,1,0:T(8,128)(2,1)} collective-permute-done((bf16[3,2048,128]{2,1,0:T(8,128)(2,1)}, bf16[3,2048,128]{2,1,0:T(8,128)(2,1)}, u32[]{:S(2)}, u32[]{:S(2)}) %collective-permute-start.4) | collective-permute-done | bytes 1572896 | tf_op jit(solution)/shard_map/ppermute | solution.py:288
  324.3 1.8 fusion
  326.1 1.7 fusion.5
  (46 shorter events, 1.1 us)
Async XLA Ops:
  7.2 1.9 copy-start.10
  12.3 13.0 %copy-start.3 = (s32[64]{0:T(128)S(1)}, s32[64]{0:T(128)}, u32[]{:S(2)}) copy-start(s32[64]{0:T(128)} %param.12) | copy-start | bytes 772
  12.3 66.7 %copy-start.2 = (f32[128,2]{0,1:T(2,128)S(1)}, f32[128,2]{0,1:T(2,128)}, u32[]{:S(2)}) copy-start(f32[128,2]{0,1:T(2,128)} %param.11) | copy-start | bytes 3076
  12.3 66.7 %copy-start.4 = (bf16[128,2048]{1,0:T(8,128)(2,1)S(1)}, bf16[128,2048]{1,0:T(8,128)(2,1)}, u32[]{:S(2)}) copy-start(bf16[128,2048]{1,0:T(8,128)(2,1)} %tokens_ref.1) | copy-start | bytes 1572868
  12.3 66.7 %copy-start.5 = (bf16[128,2048]{1,0:T(8,128)(2,1)S(1)}, bf16[128,2048]{1,0:T(8,128)(2,1)}, u32[]{:S(2)}) copy-start(bf16[128,2048]{1,0:T(8,128)(2,1)} %cot_ref.3) | copy-start | bytes 1572868
  12.3 66.7 %copy-start.6 = (s32[128,2]{0,1:T(2,128)S(1)}, s32[128,2]{0,1:T(2,128)}, u32[]{:S(2)}) copy-start(s32[128,2]{0,1:T(2,128)} %param.10) | copy-start | bytes 3076
  12.3 52.1 %all-to-all-start.2 = ((bf16[64,96,128]{2,1,0:T(8,128)(2,1)}), bf16[64,96,128]{2,1,0:T(8,128)(2,1)S(1)}, u32[]{:S(2)}, u32[]{:S(2)}) async-start(bf16[64,96,128]{2,1,0:T(8,128)(2,1)} %bitcast.18), calls=%async_computation.2 | async-start | bytes 3145728 | tf_op jit(solution)/shard_map/all_to_all | solution.py:284
  25.2 90.3 %all-gather.2.cloned.1.call-start = ((), (), s32[]{:S(2)}) async-start(), calls=%async_computation.7 | async-start | bytes 1769472 | tf_op jit(solution)/shard_map/all_gather | solution.py:311
  64.4 1.3 collective-permute-start.1
  82.8 1.3 collective-permute-start
  115.5 1.4 copy-start.1
  140.3 51.3 %all-to-all-start = ((bf16[64,8,2048]{2,1,0:T(8,128)(2,1)}), bf16[64,8,2048]{2,1,0:T(8,128)(2,1)}, u32[]{:S(2)}, u32[]{:S(2)}) async-start(bf16[64,8,2048]{2,1,0:T(8,128)(2,1)} %bitcast.4), calls=%async_computation | async-start | bytes 4194304 | tf_op jit(solution)/shard_map/all_to_all | solution.py:284
  206.9 11.5 %all-to-all-start.3 = ((bf16[4,48,2048]{2,1,0:T(8,128)(2,1)}), bf16[4,48,2048]{2,1,0:T(8,128)(2,1)S(1)}, u32[]{:S(2)}, u32[]{:S(2)}) async-start(bf16[4,48,2048]{2,1,0:T(8,128)(2,1)} %bitcast.21), calls=%async_computation.3 | async-start | bytes 1572864 | tf_op jit(solution)/shard_map/all_to_all | solution.py:284
  211.9 1.3 collective-permute-start.5
  218.4 41.2 %all-to-all-start.6 = ((bf16[64,96,128]{2,1,0:T(8,128)(2,1)}), bf16[64,96,128]{2,1,0:T(8,128)(2,1)S(1)}, u32[]{:S(2)}, u32[]{:S(2)}) async-start(bf16[64,96,128]{2,1,0:T(8,128)(2,1)} %select_select_fusion), calls=%async_computation.6 | async-start | bytes 3145728 | tf_op jit(solution)/shard_map/all_to_all | solution.py:284
  239.5 2.7 copy-start
  242.2 25.4 %collective-permute-start.3 = (bf16[2,3,2048,128]{3,2,1,0:T(8,128)(2,1)}, bf16[2,3,2048,128]{3,2,1,0:T(8,128)(2,1)}, u32[]{:S(2)}, u32[]{:S(2)}) collective-permute-start(bf16[2,3,2048,128]{3,2,1,0:T(8,128)(2,1)} %get-tuple-element.38), channel_id=1, source_target_pairs={{0,1},{1,0},{2,3},{3,2},{4,5},{5,4},{6,7},{7,6},{8,9},{9,8},{10,11... | collective-permute-start | bytes 9437192 | tf_op jit(solution)/shard_map/ppermute | solution.py:288
  259.6 1.2 copy-start.8
  260.7 52.9 %all-to-all-start.1 = ((bf16[64,8,2048]{2,1,0:T(8,128)(2,1)}), bf16[64,8,2048]{2,1,0:T(8,128)(2,1)S(1)}, u32[]{:S(2)}, u32[]{:S(2)}) async-start(bf16[64,8,2048]{2,1,0:T(8,128)(2,1)} %bitcast.6), calls=%async_computation.1 | async-start | bytes 4194304 | tf_op jit(solution)/shard_map/all_to_all | solution.py:284
  271.8 2.7 copy-start.7
  274.4 2.3 copy-start.9
  275.9 48.4 %collective-permute-start.4 = (bf16[3,2048,128]{2,1,0:T(8,128)(2,1)}, bf16[3,2048,128]{2,1,0:T(8,128)(2,1)}, u32[]{:S(2)}, u32[]{:S(2)}) collective-permute-start(bf16[3,2048,128]{2,1,0:T(8,128)(2,1)} %fusion.1), channel_id=1, source_target_pairs={{0,2},{2,0},{1,3},{3,1},{4,6},{6,4},{5,7},{7,5},{8,10},{10,8},{9,1... | collective-permute-start | bytes 4718600 | tf_op jit(solution)/shard_map/ppermute | solution.py:288
  277.7 39.4 %collective-permute-start.6 = (bf16[8,4,96,128]{3,2,1,0:T(8,128)(2,1)}, bf16[8,4,96,128]{3,2,1,0:T(8,128)(2,1)}, u32[]{:S(2)}, u32[]{:S(2)}) collective-permute-start(bf16[8,4,96,128]{3,2,1,0:T(8,128)(2,1)} %dynamic-slice_bitcast_fusion), channel_id=1, source_target_pairs={{0,1},{1,0},{2,3},{3,2},{4,5},{5,4},{6,7},{7,6},{8,9},{9,8},{10,11... | collective-permute-start | bytes 2359304 | tf_op jit(solution)/shard_map/ppermute | solution.py:288
  279.5 1.8 collective-permute-start.2
  317.1 7.2 %slice-start = ((s8[6291456]{0:T(1024)(128)(4,1)}), s8[4194304]{0:T(1024)(128)(4,1)S(1)}, s32[]{:S(2)}) async-start(s8[6291456]{0:T(1024)(128)(4,1)} %bitcast.70), calls=%async_computation.8 | async-start | bytes 8388608
  318.7 5.6 %slice-start.1 = ((s8[6291456]{0:T(1024)(128)(4,1)}), s8[2097152]{0:T(1024)(128)(4,1)S(1)}, s32[]{:S(2)}) async-start(s8[6291456]{0:T(1024)(128)(4,1)} %bitcast.70), calls=%async_computation.9 | async-start | bytes 4194304
Sparse Core Ops, SparseCore 0:
  79.1 36.3 all-gather.1
